TPU v7x, 32 devices: a whole 2x2x4 slice. The times are simulated.
32 devices in a mesh: ctx: 16 (over z, x, core), exp: 2 (over y).
Axes of the slice: x: 2, y: 2, z: 4, core: 2. Of those that a mesh axis runs over, the one named last changes fastest.
Arguments:
- queries: bfloat16 [128, 73728], P(('ctx', 'exp')), may hold values from -24 to 24
- latents: bfloat16 [1280, 576], P('ctx'), may hold values from -6 to 6
- offsets: int32 [32], P(('ctx', 'exp')), may hold values from 1152 to 1276, as said below
- moe_input: bfloat16 [64, 5120], P('exp', 'ctx'), may hold values from -6 to 6
- routes: int32 [64, 6], P('exp'), may hold values from 0 to 15, all different within a row; in each aligned block of 32 rows (0 to 31, 32 to 63, ...) at most 16 rows name the same one
- gate_values: float32 [64, 6], P('exp'), may hold values from 0.05 to 0.45
- w_gate: bfloat16 [16, 5120, 1536], P('exp', 'ctx'), may hold values from -0.078125 to 0.078125
- w_up: bfloat16 [16, 5120, 1536], P('exp', 'ctx'), may hold values from -0.078125 to 0.078125
- w_down: bfloat16 [16, 1536, 5120], P('exp', None, 'ctx'), may hold values from -0.15625 to 0.15625
Outputs:
- attention_out: bfloat16 [128, 65536], P(('ctx', 'exp'))
- moe_output: bfloat16 [64, 5120], P('exp', 'ctx')
Inputs may be any that keep to these rules, and one draw needn't show every extreme that they name: `offsets`: the query blocks start at distinct positions 1152 + k * 4, one block for each k. `routes`: each row names 6 different experts; the 32 rows of one index of exp name no expert more than 16 times, and in every draw some expert is named exactly 16 times there.
All inputs are finite; a program needn't handle non-finite values.
Results may differ from a plain program's by a relative error of at most 0.0075.
Values may be sent and summed in bfloat16 or wider, within the bound.
A program may use at most 64 MiB of HBM per device.

v0:
```python
import math

import jax
import jax.numpy as jnp
from jax import lax
from jax.sharding import PartitionSpec as P

H = 128
LAT = 512
ROPE = 64
TOPK = 6
EXPERTS = 16
CAP = 16


softmax_scale = 192.0 ** (-0.5)


def attend_keys(status, query_rows, query_pos, key_block, first_key):
    running_max, denominators, accumulated = status
    scores = (
        lax.dot_general(
            query_rows, key_block, (((1,), (1,)), ((), ())), preferred_element_type=jnp.float32
        )
        * softmax_scale
    )
    key_pos = first_key + lax.iota(jnp.int32, key_block.shape[0])
    scores = jnp.where(key_pos[None, :] <= query_pos[:, None], scores, -jnp.inf)
    new_max = jnp.maximum(running_max, jnp.max(scores, axis=1))
    rescale = jnp.exp(running_max - new_max)
    weights = jnp.exp(scores - new_max[:, None])
    denominators = denominators * rescale + jnp.sum(weights, axis=1)
    rounded = weights.astype(jnp.bfloat16)
    accumulated = accumulated * rescale[:, None] + jnp.dot(
        rounded, key_block[:, :LAT], preferred_element_type=jnp.float32
    )
    return (new_max, denominators, accumulated)


def local(queries, latents, offsets, moe_input, routes, gate_values, w_gate, w_up, w_down):
    width_all = LAT + ROPE
    row_count = queries.shape[0] * H
    query_rows = queries.reshape(row_count, width_all)
    query_pos = offsets[0] + lax.iota(jnp.int32, row_count) // H
    start_state = (
        jnp.full((row_count,), -1e30, jnp.float32),
        jnp.zeros((row_count,), jnp.float32),
        jnp.zeros((row_count, LAT), jnp.float32),
    )
    every_key = lax.all_gather(latents, "ctx", axis=0, tiled=True)
    status = start_state
    key_count = every_key.shape[0]
    span_rows = math.gcd(key_count, 640)
    stacked = every_key.reshape(key_count // span_rows, span_rows, width_all)
    firsts = 0 + span_rows * lax.iota(jnp.int32, key_count // span_rows)

    def advance(carried, inputs):
        return (attend_keys(carried, query_rows, query_pos, inputs[0], inputs[1]), None)

    status, unused = lax.scan(advance, status, (stacked, firsts))
    attention_out = (
        (status[2] / status[1][:, None]).astype(jnp.bfloat16).reshape(queries.shape[0], H * LAT)
    )
    token_count = moe_input.shape[0]
    local_width = moe_input.shape[1]
    held_experts = w_gate.shape[0]
    owner_count = lax.axis_size("exp")
    chosen = routes.reshape(-1)
    one_hot = (chosen[:, None] == lax.iota(jnp.int32, EXPERTS)[None, :]).astype(jnp.int32)
    earlier = jnp.cumsum(one_hot, axis=0) - one_hot
    slot_rank = jnp.sum(earlier * one_hot, axis=1)
    slot_index = chosen * CAP + slot_rank
    placed = (slot_index[:, None] == lax.iota(jnp.int32, EXPERTS * CAP)[None, :]).reshape(
        token_count, TOPK, EXPERTS * CAP
    )
    selector = jnp.any(placed, axis=1).astype(jnp.bfloat16)
    outgoing = lax.dot_general(
        selector, moe_input, (((0,), (0,)), ((), ())), preferred_element_type=jnp.float32
    ).astype(jnp.bfloat16)
    outgoing = outgoing.reshape(owner_count, held_experts * CAP, local_width)
    arrived = lax.all_to_all(outgoing, "exp", split_axis=0, concat_axis=0, tiled=True)
    arrived = arrived.reshape(owner_count, held_experts, CAP, local_width)
    gate_part = jnp.einsum("secd,edf->secf", arrived, w_gate, preferred_element_type=jnp.float32)
    up_part = jnp.einsum("secd,edf->secf", arrived, w_up, preferred_element_type=jnp.float32)
    gate_full, up_full = lax.psum((gate_part, up_part), "ctx")
    hidden = (jax.nn.silu(gate_full) * up_full).astype(jnp.bfloat16)
    result = jnp.einsum(
        "secf,efd->secd", hidden, w_down, preferred_element_type=jnp.float32
    ).astype(jnp.bfloat16)
    returned = lax.all_to_all(
        result.reshape(owner_count, held_experts * CAP, local_width),
        "exp",
        split_axis=0,
        concat_axis=0,
        tiled=True,
    )
    combine_weights = jnp.sum(placed.astype(jnp.float32) * gate_values[:, :, None], axis=1)
    moe_output = jnp.dot(
        combine_weights,
        returned.reshape(EXPERTS * CAP, local_width).astype(jnp.float32),
        precision=lax.Precision.HIGHEST,
    ).astype(jnp.bfloat16)
    return (attention_out, moe_output)


def solution(mesh):
    return jax.shard_map(
        local,
        mesh=mesh,
        in_specs=(
            P(("ctx", "exp"), None),
            P("ctx", None),
            P(("ctx", "exp")),
            P("exp", "ctx"),
            P("exp", None),
            P("exp", None),
            P("exp", "ctx", None),
            P("exp", "ctx", None),
            P("exp", None, "ctx"),
        ),
        out_specs=(P(("ctx", "exp"), None), P("exp", "ctx")),
        check_vma=False,
    )
```

profile of v0, /device:TPU:0, one launch (start us, length us, event | category | flops | bytes accessed | tf_op | source)
XLA Modules:
  0.0 191.1 jit_solution(12343541402807582805)
XLA Ops:
  7.2 0.8 copy.56
  8.1 0.6 reduce-window.6
  9.2 0.7 multiply_add_fusion
  10.1 0.2 fusion.32
  10.3 8.7 %all_to_all.10 = bf16[2,128,320]{1,2,0:T(8,128)(2,1)S(1)} all-to-all(bf16[2,128,320]{1,2,0:T(8,128)(2,1)S(1)} %bitcast.81), channel_id=1, replica_groups=mesh['ctx'=16,'exp'=2] {'exp'}, dimensions={0} | all-to-all | bytes 327680 | tf_op jit(solution)/shard_map/all_to_all | solution.py:81
  19.2 5.9 %fusion.20 = f32[2,8,16,1536]{3,2,0,1:T(8,128)} fusion(bf16[8,320,1536]{2,1,0:T(8,128)(2,1)} %param.17, bf16[2,8,16,320]{3,2,1,0:T(8,128)(2,1)S(1)} %bitcast.78), kind=kOutput, calls=%fused_computation.31 | convolution fusion | flops 251658240 | bytes 9601024 | tf_op jit(solution)/shard_map/secd,edf->secf/dot_general | solution.py:83
  25.1 2.6 %fusion.23 = f32[2,8,16,1536]{3,2,0,1:T(8,128)} fusion(bf16[8,320,1536]{2,1,0:T(8,128)(2,1)S(1)} %copy-done.1, bf16[2,8,16,320]{3,2,1,0:T(8,128)(2,1)S(1)} %bitcast.79), kind=kOutput, calls=%fused_computation.32 | convolution fusion | flops 251658240 | bytes 9601024 | tf_op jit(solution)/shard_map/secd,edf->secf/dot_general | solution.py:84
  27.8 0.7 all-gather.2.cloned.1.call-update
  28.5 0.3 copy-done.3
  28.8 1.6 reshape.65
  30.5 101.3 %all-reduce.4.cloned.1.call-done = (f32[2,8,16,1536]{3,2,0,1:T(8,128)}, f32[2,8,16,1536]{3,2,0,1:T(8,128)}) async-done(((f32[2,8,16,1536]{3,2,0,1:T(8,128)}, f32[2,8,16,1536]{3,2,0,1:T(8,128)}), (f32[2,8,16,1536]{3,2,0,1:T(8,128)}, f32[2,8,16,1536]{3,2,0,1:T(8,128)})) %all-reduce.4.cloned.1.call-update) | async-done | bytes 3145744 | tf_op jit(solution)/shard_map/psum | solution.py:85
  131.8 6.3 %fusion.29 = bf16[2,8,16,320]{3,2,0,1:T(8,128)(2,1)S(1)} fusion(bf16[8,1536,320]{1,2,0:T(8,128)(2,1)} %param.19, f32[2,8,16,1536]{3,2,0,1:T(8,128)} %get-tuple-element.93, f32[2,8,16,1536]{3,2,0,1:T(8,128)} %get-tuple-element.94), kind=kOutput, calls=%fused_computation.36 | convolution fusion | flops 254099456 | bytes 11173888 | tf_op jit(solution)/shard_map/secf,efd->secd/dot_general | solution.py:87
  138.2 0.8 copy.65
  139.0 3.4 %all-to-all-start.1 = ((bf16[2,128,320]{1,2,0:T(8,128)(2,1)}), bf16[2,128,320]{1,2,0:T(8,128)(2,1)S(1)}, u32[]{:S(2)}, u32[]{:S(2)}) async-start(bf16[2,128,320]{1,2,0:T(8,128)(2,1)} %copy.65), calls=%async_computation.1 | async-start | bytes 327680 | tf_op jit(solution)/shard_map/all_to_all | solution.py:90
  142.4 4.6 %all-to-all-done.1 = bf16[2,128,320]{1,2,0:T(8,128)(2,1)S(1)} async-done(((bf16[2,128,320]{1,2,0:T(8,128)(2,1)}), bf16[2,128,320]{1,2,0:T(8,128)(2,1)S(1)}, u32[]{:S(2)}, u32[]{:S(2)}) %all-to-all-start.1) | async-done | bytes 163872 | tf_op jit(solution)/shard_map/all_to_all | solution.py:90
  147.0 0.9 convolution_convert_fusion.1
  147.9 25.2 %all-gather.2.cloned.1.call-done = bf16[1280,576]{1,0:T(8,128)(2,1)} async-done(((bf16[80,576]{1,0:T(8,128)(2,1)}), bf16[1280,576]{1,0:T(8,128)(2,1)}) %all-gather.2.cloned.1.call-update) | async-done | bytes 1474576 | tf_op jit(solution)/shard_map/all_gather | solution.py:50
  173.1 9.8 %while.15 = (s32[]{:T(128)}, f32[512]{0:T(512)S(1)}, f32[512]{0:T(512)S(1)}, f32[512,512]{1,0:T(8,128)S(1)}, s32[2]{0:T(128)S(1)}, /*index=5*/bf16[2,640,576]{2,...) while((s32[]{:T(128)}, f32[512]{0:T(512)S(1)}, f32[512]{0:T(512)S(1)}, ...), condition=%wide.region_3.4_spmd.clone, body=%wide.region_0.3_spmd.clone.sunk | while | flops 716447360 | bytes 11887781 | solution.py:60
  173.1 1.3 dynamic-slice_bitcast_fusion.2
  174.4 0.6 dynamic_slice.14
  175.0 0.6 iota_add_fusion.2
  175.7 0.7 fusion.61
  176.3 0.7 fusion.62
  177.1 0.2 fusion.63
  177.3 0.6 convolution_add_fusion.2
  178.0 1.3 dynamic-slice_bitcast_fusion.2
  179.3 0.6 dynamic_slice.14
  179.9 0.6 iota_add_fusion.2
  180.6 0.7 fusion.61
  181.2 0.7 fusion.62
  182.2 0.6 convolution_add_fusion.2
  183.1 1.2 reshape.66
  (41 shorter events, 1.6 us)
Async XLA Ops:
  7.2 2.9 %copy-start = (bf16[32,320]{1,0:T(8,128)(2,1)S(1)}, bf16[32,320]{1,0:T(8,128)(2,1)}, u32[]{:S(2)}) copy-start(bf16[32,320]{1,0:T(8,128)(2,1)} %param.14) | copy-start | bytes 61444
  7.2 124.6 %all-reduce.4.cloned.1.call-start = ((), (), s32[]{:S(2)}) async-start(), calls=%async_computation.3 | async-start | bytes 6291456 | tf_op jit(solution)/shard_map/psum | solution.py:85
  19.2 6.0 %copy-start.1 = (bf16[8,320,1536]{2,1,0:T(8,128)(2,1)S(1)}, bf16[8,320,1536]{2,1,0:T(8,128)(2,1)}, u32[]{:S(2)}) copy-start(bf16[8,320,1536]{2,1,0:T(8,128)(2,1)} %param.18) | copy-start | bytes 23592964
  27.7 1.1 copy-start.3
  27.7 2.6 %copy-start.4 = (f32[32,6]{0,1:T(8,128)S(1)}, f32[32,6]{0,1:T(8,128)}, u32[]{:S(2)}) copy-start(f32[32,6]{0,1:T(8,128)} %param.16) | copy-start | bytes 2308
  27.8 145.4 %all-gather.2.cloned.1.call-start = ((), (), s32[]{:S(2)}) async-start(), calls=%async_computation.2 | async-start | bytes 1740800 | tf_op jit(solution)/shard_map/all_gather | solution.py:50
  139.0 8.1 %all-to-all-start.1 = ((bf16[2,128,320]{1,2,0:T(8,128)(2,1)}), bf16[2,128,320]{1,2,0:T(8,128)(2,1)S(1)}, u32[]{:S(2)}, u32[]{:S(2)}) async-start(bf16[2,128,320]{1,2,0:T(8,128)(2,1)} %copy.65), calls=%async_computation.1 | async-start | bytes 327680 | tf_op jit(solution)/shard_map/all_to_all | solution.py:90
  173.1 3.2 %copy-start.2 = (bf16[512,576]{1,0:T(8,128)(2,1)S(1)}, bf16[512,576]{1,0:T(8,128)(2,1)}, u32[]{:S(2)}) copy-start(bf16[512,576]{1,0:T(8,128)(2,1)} %get-tuple-element.182) | copy-start | bytes 1769476 | tf_op jit(solution)/shard_map/while
  178.0 3.2 %copy-start.2 = (bf16[512,576]{1,0:T(8,128)(2,1)S(1)}, bf16[512,576]{1,0:T(8,128)(2,1)}, u32[]{:S(2)}) copy-start(bf16[512,576]{1,0:T(8,128)(2,1)} %get-tuple-element.182) | copy-start | bytes 1769476 | tf_op jit(solution)/shard_map/while
Sparse Core Ops, SparseCore 0:
  27.9 103.8 all-reduce.3
  133.9 39.1 all-gather.1
where the time goes:
time: 192 us; the launch traced here: 191 us
  waiting for transfers between devices  132 us (69%)
  matrix products  18.7 us (10%)
  between operations  14.2 us (7%)
  local copies, waits for them, and re-layouts  9.05 us (5%)
  blocking collectives  8.68 us (5%)
  other arithmetic  4.91 us (3%)
  starting transfers between devices  3.51 us (2%)
    psum x1, waiting for transfers between devices, local(): gate_full, up_full = lax.psum((gate_part, up_part), 'ctx')  101 us
    all_gather x1, waiting for transfers between devices, local(): every_key = lax.all_gather(latents, 'ctx', axis=0, tiled=True)  25.2 us
    all_to_all x1, blocking collectives, local(): lax.all_to_all(outgoing, 'exp', split_axis=0, concat_axis=0, tiled=True)  8.68 us
    dot_general x1, matrix products, local(): jnp.einsum('secf,efd->secd', hidden, w_down, preferred_element_type=jnp.f...  6.34 us
    dot_general x1, matrix products, local(): jnp.einsum('secd,edf->secf', arrived, w_gate, preferred_element_type=jnp....  5.95 us
    all_to_all x1, waiting for transfers between devices, local(): lax.all_to_all(result.reshape(owner_count, held_experts * CAP, local_widt...  4.62 us
  transfers between devices with their start and end apart: 3, of which 3 were waited for; matrix products, arithmetic and copies ran while one was open for 5% of the time, Pallas kernels for 0%

commit v1 on v0

v1 whole, which is shorter than its diff:
```python
import functools

import jax
import jax.numpy as jnp
from jax import lax
from jax.experimental import pallas as pl
from jax.experimental.pallas import tpu as pltpu
from jax.sharding import PartitionSpec as P

H = 128
LAT = 512
ROPE = 64
TOPK = 6
EXPERTS = 16
CAP = 16
MESH = pl.DeviceIdType.MESH

softmax_scale = 192.0 ** (-0.5)


def attend_kernel(offset_ref, query_ref, key_ref, out_ref):
    keys = key_ref[...]
    values = key_ref[:, :LAT]
    key_pos = lax.broadcasted_iota(jnp.int32, (1, keys.shape[0]), 1)

    @pl.loop(0, query_ref.shape[0] // H)
    def _(token):
        rows = pl.ds(pl.multiple_of(token * H, H), H)
        scores = (
            lax.dot_general(
                query_ref[rows, :], keys, (((1,), (1,)), ((), ())), preferred_element_type=jnp.float32
            )
            * softmax_scale
        )
        scores = jnp.where(key_pos <= offset_ref[0] + token, scores, -jnp.inf)
        weights = jnp.exp(scores - jnp.max(scores, axis=1, keepdims=True))
        denominator = jnp.sum(weights, axis=1, keepdims=True)
        mixed = jnp.dot(weights.astype(jnp.bfloat16), values, preferred_element_type=jnp.float32)
        out_ref[rows, :] = (mixed / denominator).astype(out_ref.dtype)


def attend(queries, every_key, offsets):
    rows = queries.shape[0] * H
    out = pl.pallas_call(
        attend_kernel,
        out_shape=jax.ShapeDtypeStruct((rows, LAT), jnp.bfloat16),
        in_specs=[
            pl.BlockSpec(memory_space=pltpu.SMEM),
            pl.BlockSpec(memory_space=pltpu.VMEM),
            pl.BlockSpec(memory_space=pltpu.VMEM),
        ],
        out_specs=pl.BlockSpec(memory_space=pltpu.VMEM),
        compiler_params=pltpu.CompilerParams(vmem_limit_bytes=32 * 2**20),
        cost_estimate=pl.CostEstimate(
            flops=2 * rows * every_key.shape[0] * (2 * LAT + ROPE),
            bytes_accessed=rows * (2 * LAT + ROPE) * 2 + every_key.size * 2,
            transcendentals=rows * every_key.shape[0],
        ),
        name="attend",
    )(offsets, queries.reshape(rows, LAT + ROPE), every_key)
    return out.reshape(queries.shape[0], H * LAT)


def expert_kernel(
    n, owners,
    table_ref, tokens_ref, gate_hbm, up_hbm, down_hbm, out_ref,
    gate_w, up_w, down_w, w_sem,
    tables, tokens, t_ssem, t_rsem, x_rows,
    keep, core_send, core_recv, c_ssem, c_rsem,
    side_send, side_recv, s_ssem, s_rsem,
    far_send, far_recv, own, f_ssem, f_rsem,
    hidden, hz_ssem, hz_rsem, hx_ssem, hx_rsem, hc_ssem, hc_rsem,
    result, back_send, back_recv, b_ssem, b_rsem,
):
    held = gate_hbm.shape[0]
    ff = gate_hbm.shape[2]
    count = tokens_ref.shape[0]
    rows = owners * CAP
    half = rows // 2
    pairs = held // 2
    nz = n // 4
    subs = nz // pairs
    row_blocks = half // 16
    col_blocks = subs // row_blocks
    width = ff // col_blocks

    ctx = lax.axis_index("ctx")
    exp = lax.axis_index("exp")
    core = lax.rem(ctx, 2)
    side = lax.rem(ctx // 2, 2)
    far = ctx // 4
    sibling = (ctx + 1 - 2 * core, exp)
    beside = (ctx + 2 - 4 * side, exp)

    def at_far(index):
        return (index * 4 + side * 2 + core, exp)

    def far_of(step):
        return lax.rem(far + step, nz)

    def owner_of(step):
        return lax.rem(exp + step, owners)

    pair_of = [lax.rem(far // subs + 1 + i, pairs) for i in range(pairs)]
    weight_copies = {}
    for i in range(pairs):
        for j in range(2):
            expert = pair_of[i] * 2 + (1 - side if j == 0 else side)
            weight_copies[i, j] = [
                pltpu.make_async_copy(hbm.at[expert], vmem.at[expert], w_sem.at[k, i, j])
                for k, (hbm, vmem) in enumerate(((gate_hbm, gate_w), (up_hbm, up_w)))
            ]
            for copy in weight_copies[i, j]:
                copy.start()
    down_order = [(d, j) for d in range(pairs) for j in range(2)]
    down_expert = {}
    down_copies = {}
    for d, j in down_order:
        expert = lax.rem(far // subs + d, pairs) * 2 + (side if j == 0 else 1 - side)
        down_expert[d, j] = expert
        down_copies[d, j] = pltpu.make_async_copy(
            down_hbm.at[expert], down_w.at[expert], w_sem.at[2, d, j]
        )
        down_copies[d, j].start()

    barrier = pltpu.get_barrier_semaphore()
    greeted = [sibling, beside]
    greeted += [at_far(far_of(k)) for k in range(1, nz)]
    greeted += [(ctx, owner_of(k)) for k in range(1, owners)]
    for device in greeted:
        pl.semaphore_signal(barrier, inc=1, device_id=device, device_id_type=MESH)
    pl.semaphore_wait(barrier, len(greeted))

    sent = []

    def send(src, dst, ssem, rsem, device):
        copy = pltpu.make_async_remote_copy(
            src_ref=src, dst_ref=dst, send_sem=ssem, recv_sem=rsem,
            device_id=device, device_id_type=MESH,
        )
        copy.start()
        sent.append(copy)

    def arrived(dst, sem):
        pltpu.make_async_remote_copy(
            src_ref=dst, dst_ref=dst, send_sem=sem, recv_sem=sem,
            device_id=sibling, device_id_type=MESH,
        ).wait_recv()

    for k in range(1, owners):
        device = (ctx, owner_of(k))
        send(table_ref, tables.at[exp], t_ssem.at[0, k], t_rsem.at[0, exp], device)
        send(tokens_ref, tokens.at[exp], t_ssem.at[1, k], t_rsem.at[1, exp], device)

    first = exp * held
    expert_ids = (lax.broadcasted_iota(jnp.int32, (held, count), 0) + first).astype(jnp.float32)
    earlier = (
        lax.broadcasted_iota(jnp.int32, (count, count), 0)
        < lax.broadcasted_iota(jnp.int32, (count, count), 1)
    ).astype(jnp.bfloat16)
    slots = lax.broadcasted_iota(jnp.int32, (held, CAP, count), 1).astype(jnp.float32)

    def placement(table):
        named = jnp.zeros((held, count), jnp.float32)
        gates = jnp.zeros((held, count), jnp.float32)
        for k in range(TOPK):
            hit = table[k : k + 1, :count] == expert_ids
            named = jnp.where(hit, 1.0, named)
            gates = jnp.where(hit, table[8 + k : 9 + k, :count], gates)
        rank = jnp.dot(named.astype(jnp.bfloat16), earlier, preferred_element_type=jnp.float32)
        rank = jnp.where(named > 0.5, rank, -1.0)
        picked = rank[:, None, :] == slots
        chosen = jnp.where(picked, 1.0, 0.0).reshape(held * CAP, count)
        weighted = jnp.where(picked, gates[:, None, :], 0.0).reshape(held * CAP, count)
        return chosen.astype(jnp.bfloat16), weighted

    def place(table, values, owner):
        chosen, weighted = placement(table)
        placed = jnp.dot(chosen, values, preferred_element_type=jnp.float32).astype(jnp.bfloat16)
        for e in range(held):
            x_rows[e, pl.ds(pl.multiple_of(owner * CAP, CAP), CAP), :] = placed[e * CAP : (e + 1) * CAP]
        return weighted

    weighted_of = {0: place(table_ref[...], tokens_ref[...], exp)}
    for k in range(1, owners):
        owner = owner_of(k)
        arrived(tables.at[owner], t_rsem.at[0, owner])
        arrived(tokens.at[owner], t_rsem.at[1, owner])
        weighted_of[k] = place(tables[owner], tokens[owner], owner)

    mine = pl.ds(pl.multiple_of(core * half, 16), half)
    other = pl.ds(pl.multiple_of((1 - core) * half, 16), half)

    def multiply(i):
        for j in range(2):
            expert = pair_of[i] * 2 + (1 - side if j == 0 else side)
            for k, weight in ((0, gate_w), (1, up_w)):
                weight_copies[i, j][k].wait()
                columns = slice(k * ff, (k + 1) * ff)
                held_w = weight[expert]
                core_send[i, j, :, columns] = jnp.dot(
                    x_rows[expert, other, :], held_w, preferred_element_type=jnp.float32
                ).astype(jnp.bfloat16)
                keep[i, j, :, columns] = jnp.dot(
                    x_rows[expert, mine, :], held_w, preferred_element_type=jnp.float32
                )
            send(core_send.at[i, j], core_recv.at[i, j], c_ssem.at[i, j], c_rsem.at[i, j], sibling)

    def to_side(i):
        arrived(core_recv.at[i, 0], c_rsem.at[i, 0])
        side_send[i] = (keep[i, 0] + core_recv[i, 0].astype(jnp.float32)).astype(jnp.bfloat16)
        send(side_send.at[i], side_recv.at[i], s_ssem.at[i], s_rsem.at[i], beside)

    def block(i, sub):
        row = lax.rem(sub, row_blocks)
        return i, row, sub // row_blocks

    def to_far(i):
        arrived(core_recv.at[i, 1], c_rsem.at[i, 1])
        arrived(side_recv.at[i], s_rsem.at[i])
        total = (
            keep[i, 1] + core_recv[i, 1].astype(jnp.float32) + side_recv[i].astype(jnp.float32)
        )
        for r in range(row_blocks):
            for c in range(col_blocks):
                for k in range(2):
                    piece = total[r * 16 : r * 16 + 16, k * ff + c * width : k * ff + (c + 1) * width]
                    at = c * row_blocks + r
                    far_send[i, at, :, k * width : (k + 1) * width] = piece.astype(jnp.bfloat16)
                    if i == pairs - 1:
                        own[at, :, k * width : (k + 1) * width] = piece
        my_sub = lax.rem(far, subs)
        for s in range(subs if i < pairs - 1 else subs - 1):
            sub = lax.rem(my_sub + 1 + s, subs)
            dest = pair_of[i] * subs + sub
            send(
                far_send.at[i, sub], far_recv.at[far], f_ssem.at[i, s], f_rsem.at[far], at_far(dest)
            )

    for t in range(pairs + 2):
        if t < pairs:
            multiply(t)
        if 0 <= t - 1 < pairs:
            to_side(t - 1)
        if 0 <= t - 2 < pairs:
            to_far(t - 2)

    total = own[lax.rem(far, subs)]
    for k in range(1, nz):
        sender = far_of(nz - k)
        arrived(far_recv.at[sender], f_rsem.at[sender])
        total = total + far_recv[sender].astype(jnp.float32)
    gate, up = total[:, :width], total[:, width:]
    hidden[far, side, core] = (gate / (1.0 + jnp.exp(-gate)) * up).astype(jnp.bfloat16)

    def pass_on(where, slot_side, ssems, rsems, device):
        here = hidden.at[where, slot_side, core]
        send(here, here, ssems, rsems, device)

    mine_block = hidden.at[far, side, core]
    for k in range(1, nz):
        send(mine_block, mine_block, hz_ssem.at[k], hz_rsem.at[far], at_far(far_of(k)))
    for k in range(nz):
        where = far_of(nz - k) if k else far
        if k:
            arrived(hidden.at[where, side, core], hz_rsem.at[where])
        pass_on(where, side, hx_ssem.at[k], hx_rsem.at[where], beside)
        pass_on(where, side, hc_ssem.at[0, k], hc_rsem.at[0, where], sibling)
    for k in range(nz):
        where = far_of(nz - k) if k else far
        arrived(hidden.at[where, 1 - side, core], hx_rsem.at[where])
        pass_on(where, 1 - side, hc_ssem.at[1, k], hc_rsem.at[1, where], sibling)

    for j in range(2):
        slot_side = side if j == 0 else 1 - side
        for d in range(pairs):
            expert = down_expert[d, j]
            pair = lax.rem(far // subs + d, pairs)
            for s in range(subs):
                where = pair * subs + s
                arrived(hidden.at[where, slot_side, 1 - core], hc_rsem.at[j, where])
            strips = []
            for c in range(2):
                for r in range(row_blocks):
                    strips.append(
                        jnp.concatenate(
                            [
                                hidden[pair * subs + q * row_blocks + r, slot_side, c]
                                for q in range(col_blocks)
                            ],
                            axis=1,
                        )
                    )
            down_copies[d, j].wait()
            made = jnp.dot(
                jnp.concatenate(strips, axis=0), down_w[expert], preferred_element_type=jnp.float32
            ).astype(jnp.bfloat16)
            for s in range(owners):
                result[s, pl.ds(pl.multiple_of(expert * CAP, CAP), CAP), :] = made[
                    s * CAP : (s + 1) * CAP
                ]

    def combine(k):
        weighted = weighted_of[k]
        high = weighted.astype(jnp.bfloat16)
        rest = weighted - high.astype(jnp.float32)
        middle = rest.astype(jnp.bfloat16)
        low = (rest - middle.astype(jnp.float32)).astype(jnp.bfloat16)
        rows_back = result[owner_of(k)]
        return sum(
            lax.dot_general(
                part, rows_back, (((0,), (0,)), ((), ())), preferred_element_type=jnp.float32
            )
            for part in (low, middle, high)
        )

    for k in range(1, owners):
        back_send[k] = combine(k)
        send(
            back_send.at[k], back_recv.at[exp], b_ssem.at[k], b_rsem.at[exp], (ctx, owner_of(k))
        )
    answer = combine(0)
    for k in range(1, owners):
        owner = owner_of(k)
        arrived(back_recv.at[owner], b_rsem.at[owner])
        answer = answer + back_recv[owner]
    out_ref[...] = answer.astype(out_ref.dtype)
    for copy in sent:
        copy.wait_send()


def experts(moe_input, routes, gate_values, w_gate, w_up, w_down):
    n, owners = lax.axis_size("ctx"), lax.axis_size("exp")
    held, depth, ff = w_gate.shape
    count, local_width = moe_input.shape
    pad = ((0, 8 - TOPK), (0, 128 - count))
    table = jnp.concatenate(
        [jnp.pad(routes.T.astype(jnp.float32), pad), jnp.pad(gate_values.T, pad)], axis=0
    )
    half = owners * CAP // 2
    pairs = held // 2
    nz = n // 4
    subs = nz // pairs
    width = ff * (half // 16) // subs
    dma = pltpu.SemaphoreType.DMA
    bf16, f32 = jnp.bfloat16, jnp.float32
    vm = pltpu.VMEM
    scratch = [
        vm((held, depth, ff), bf16), vm((held, depth, ff), bf16), vm((held, ff, depth), bf16),
        dma((3, pairs, 2)),
        vm((owners, 16, 128), f32), vm((owners, count, local_width), bf16),
        dma((2, owners)), dma((2, owners)),
        vm((held, owners * CAP, local_width), bf16),
        vm((pairs, 2, half, 2 * ff), f32), vm((pairs, 2, half, 2 * ff), bf16),
        vm((pairs, 2, half, 2 * ff), bf16), dma((pairs, 2)), dma((pairs, 2)),
        vm((pairs, half, 2 * ff), bf16), vm((pairs, half, 2 * ff), bf16), dma((pairs,)), dma((pairs,)),
        vm((pairs, subs, 16, 2 * width), bf16), vm((nz, 16, 2 * width), bf16),
        vm((subs, 16, 2 * width), f32), dma((pairs, subs)), dma((nz,)),
        vm((nz, 2, 2, 16, width), bf16),
        dma((nz,)), dma((nz,)), dma((nz,)), dma((nz,)), dma((2, nz)), dma((2, nz)),
        vm((owners, held * CAP, local_width), bf16),
        vm((owners, count, local_width), f32), vm((owners, count, local_width), f32),
        dma((owners,)), dma((owners,)),
    ]
    any_space = pl.BlockSpec(memory_space=pl.ANY)
    in_vmem = pl.BlockSpec(memory_space=pltpu.VMEM)
    return pl.pallas_call(
        functools.partial(expert_kernel, n, owners),
        out_shape=jax.ShapeDtypeStruct(moe_input.shape, moe_input.dtype),
        in_specs=[in_vmem, in_vmem, any_space, any_space, any_space],
        out_specs=in_vmem,
        scratch_shapes=scratch,
        compiler_params=pltpu.CompilerParams(
            collective_id=0, has_side_effects=True, vmem_limit_bytes=56 * 2**20
        ),
        cost_estimate=pl.CostEstimate(
            flops=6 * held * owners * CAP * depth * ff,
            bytes_accessed=3 * held * depth * ff * 2,
            transcendentals=0,
        ),
        name="experts",
    )(table, moe_input, w_gate, w_up, w_down)


def local(queries, latents, offsets, moe_input, routes, gate_values, w_gate, w_up, w_down):
    every_key = lax.all_gather(latents, "ctx", axis=0, tiled=True)
    moe_output = experts(moe_input, routes, gate_values, w_gate, w_up, w_down)
    attention_out = attend(queries, every_key, offsets)
    return (attention_out, moe_output)


def solution(mesh):
    return jax.shard_map(
        local,
        mesh=mesh,
        in_specs=(
            P(("ctx", "exp"), None),
            P("ctx", None),
            P(("ctx", "exp")),
            P("exp", "ctx"),
            P("exp", None),
            P("exp", None),
            P("exp", "ctx", None),
            P("exp", "ctx", None),
            P("exp", None, "ctx"),
        ),
        out_specs=(P(("ctx", "exp"), None), P("exp", "ctx")),
        check_vma=False,
    )
```

time: 192 us -> 86.7 us (0.45)
  waiting for transfers between devices: 132 us -> 0.7 us
  Pallas kernels: 0 us -> 53.8 us
  matrix products: 18.7 us -> 0 us
  blocking collectives: 8.68 us -> 0 us
  local copies, waits for them, and re-layouts: 9.05 us -> 16.3 us
  other arithmetic: 4.91 us -> 0.61 us
  starting transfers between devices: 3.51 us -> 0.04 us
    psum x1 -> x0, waiting for transfers between devices: 101 us -> none  [local(): gate_full, up_full = lax.psum((gate_part, up_part), 'ctx')]
    pallas_call x0 -> x2, Pallas kernels: none -> 53.8 us  [the longest x1 49.5 us: experts(): pl.pallas_call(functools.partial(expert_kernel, n, owners), out_shape=jax...]
    all_gather x1, waiting for transfers between devices: 25.2 us -> 0.02 us  [local(): every_key = lax.all_gather(latents, 'ctx', axis=0, tiled=True)]
    dot_general x9 -> x0, matrix products: 18.7 us -> none  [the longest x1 6.34 us: local(): jnp.einsum('secf,efd->secd', hidden, w_down, preferred_element_type=jnp.f...]
    unnamed x9 -> x10, local copies, waits for them, and re-layouts: 1.05 us -> 14.5 us
    all_to_all x1 -> x0, blocking collectives: 8.68 us -> none  [local(): lax.all_to_all(outgoing, 'exp', split_axis=0, concat_axis=0, tiled=True)]
    all_to_all x1 -> x0, waiting for transfers between devices: 4.62 us -> none  [local(): lax.all_to_all(result.reshape(owner_count, held_experts * CAP, local_widt...]
    all_to_all x1 -> x0, starting transfers between devices: 3.43 us -> none  [local(): lax.all_to_all(result.reshape(owner_count, held_experts * CAP, local_widt...]
  transfers between devices with their start and end apart: 3 -> 1, of which waited for: 3 -> 0; matrix products, arithmetic and copies ran while one was open for 5% -> 15% of each run, Pallas kernels for 0% -> 57%
where the time goes in v1:
time: 86.7 us; the launch traced here: 86.2 us
  Pallas kernels  53.8 us (62%)
  local copies, waits for them, and re-layouts  16.3 us (19%)
  between operations  14.7 us (17%)
    pallas_call x1, Pallas kernels, experts(): pl.pallas_call(functools.partial(expert_kernel, n, owners), out_shape=jax...  49.5 us
    unnamed x10, local copies, waits for them, and re-layouts  14.5 us
    pallas_call x1, Pallas kernels, attend(): pl.pallas_call(attend_kernel, out_shape=jax.ShapeDtypeStruct((rows, LAT),...  4.34 us
  transfers between devices with their start and end apart: 1, of which 0 were waited for; matrix products, arithmetic and copies ran while one was open for 15% of the time, Pallas kernels for 57%

profile of v1, /device:TPU:0, one launch (start us, length us, event | category | flops | bytes accessed | tf_op | source)
XLA Modules:
  0.0 86.2 jit_solution(8863587015380610519)
XLA Ops:
  7.2 0.0 all-gather.2.cloned.1.call-start
  7.2 0.7 all-gather.2.cloned.1.call-update
  7.9 0.0 copy-start.2
  7.9 0.0 copy-start.3
  7.9 11.7 %copy.12.down_hbm = bf16[8,1536,320]{2,1,0:T(8,128)(2,1)} copy(bf16[8,1536,320]{1,2,0:T(8,128)(2,1)} %param.17) | data formatting | bytes 15728640 | tf_op args[8]
  19.6 0.0 copy-done.2
  19.6 0.0 copy-done.3
  19.6 0.6 select_maximum_fusion.table_ref
  20.2 0.0 copy-start.1
  20.2 49.5 %experts.1 = bf16[32,320]{1,0:T(8,128)(2,1)} custom-call(f32[16,128]{1,0:T(8,128)} %select_maximum_fusion.table_ref, bf16[32,320]{1,0:T(8,128)(2,1)} %tokens_ref.1, bf16[8,320,1536]{2,1,0:T(8,128)(2,1)} %gate_hbm.1, bf16[8,320,1536]{2,1,0:T(8,128)(2,1)} %up_hbm.1, bf16[8,1536,320]{2,1,0:T(8,128)(2,1)} %copy.12.down_hbm), custom_call_target="tpu_custom_call" | custom-call | flops 754974720 | bytes 23592960 | tf_op jit(solution)/shard_map/experts/pallas_call | solution.py:367
  69.7 0.0 copy-done.1
  69.7 0.7 reshape.10.query_ref
  71.0 0.0 all-gather.2.cloned.1.call-done.key_ref
  71.0 0.0 copy-start
  71.1 1.4 %copy-done = bf16[1280,576]{1,0:T(8,128)(2,1)S(1)} copy-done((bf16[1280,576]{1,0:T(8,128)(2,1)S(1)}, bf16[1280,576]{1,0:T(8,128)(2,1)}, u32[]{:S(2)}) %copy-start) | copy-done | bytes 1474584
  72.5 4.3 %attend.1 = bf16[512,512]{1,0:T(8,128)(2,1)S(1)} custom-call(s32[1]{0:T(128)S(6)} %copy.14.offset_ref, bf16[512,576]{1,0:T(8,128)(2,1)S(1)} %reshape.10.query_ref, bf16[1280,576]{1,0:T(8,128)(2,1)S(1)} %copy-done), custom_call_target="tpu_custom_call" | custom-call | flops 1426063360 | bytes 2588672 | tf_op jit(solution)/shard_map/attend/pallas_call | solution.py:44
  76.8 1.2 %reshape.11 = bf16[4,65536]{1,0:T(4,128)(2,1)} reshape(bf16[512,512]{1,0:T(8,128)(2,1)S(1)} %attend.1) | data formatting | bytes 1048576 | tf_op jit(solution)/shard_map/reshape | solution.py:61
  78.0 1.3 %copy.15 = bf16[32,320]{1,0:T(8,128)(2,1)} copy(bf16[32,320]{1,0:T(8,128)(2,1)} %experts.1) | data formatting | bytes 40960
  (1 shorter events, 0.0 us)
Async XLA Ops:
  7.2 63.9 %all-gather.2.cloned.1.call-start = ((), (), s32[]{:S(2)}) async-start(), calls=%async_computation | async-start | bytes 1740800 | tf_op jit(solution)/shard_map/all_gather | solution.py:386
  7.9 11.7 %copy-start.2 = (s32[32,6]{0,1:T(8,128)S(1)}, s32[32,6]{0,1:T(8,128)}, u32[]{:S(2)}) copy-start(s32[32,6]{0,1:T(8,128)} %param.13) | copy-start | bytes 2308
  7.9 11.7 %copy-start.3 = (f32[32,6]{0,1:T(8,128)S(1)}, f32[32,6]{0,1:T(8,128)}, u32[]{:S(2)}) copy-start(f32[32,6]{0,1:T(8,128)} %param.14) | copy-start | bytes 2308
  20.2 49.5 %copy-start.1 = (bf16[4,73728]{1,0:T(4,128)(2,1)S(1)}, bf16[4,73728]{1,0:T(4,128)(2,1)}, u32[]{:S(2)}) copy-start(bf16[4,73728]{1,0:T(4,128)(2,1)} %param.9) | copy-start | bytes 1769476
  71.0 1.4 %copy-start = (bf16[1280,576]{1,0:T(8,128)(2,1)S(1)}, bf16[1280,576]{1,0:T(8,128)(2,1)}, u32[]{:S(2)}) copy-start(bf16[1280,576]{1,0:T(8,128)(2,1)} %all-gather.2.cloned.1.call-done.key_ref) | copy-start | bytes 4423684
Sparse Core Ops, SparseCore 0:
  10.2 46.3 all-gather.1

commit v2 on v1

--- a/solution.py
+++ b/solution.py
@@ -18,52 +18,11 @@
 softmax_scale = 192.0 ** (-0.5)
 
 
-def attend_kernel(offset_ref, query_ref, key_ref, out_ref):
-    keys = key_ref[...]
-    values = key_ref[:, :LAT]
-    key_pos = lax.broadcasted_iota(jnp.int32, (1, keys.shape[0]), 1)
-
-    @pl.loop(0, query_ref.shape[0] // H)
-    def _(token):
-        rows = pl.ds(pl.multiple_of(token * H, H), H)
-        scores = (
-            lax.dot_general(
-                query_ref[rows, :], keys, (((1,), (1,)), ((), ())), preferred_element_type=jnp.float32
-            )
-            * softmax_scale
-        )
-        scores = jnp.where(key_pos <= offset_ref[0] + token, scores, -jnp.inf)
-        weights = jnp.exp(scores - jnp.max(scores, axis=1, keepdims=True))
-        denominator = jnp.sum(weights, axis=1, keepdims=True)
-        mixed = jnp.dot(weights.astype(jnp.bfloat16), values, preferred_element_type=jnp.float32)
-        out_ref[rows, :] = (mixed / denominator).astype(out_ref.dtype)
-
-
-def attend(queries, every_key, offsets):
-    rows = queries.shape[0] * H
-    out = pl.pallas_call(
-        attend_kernel,
-        out_shape=jax.ShapeDtypeStruct((rows, LAT), jnp.bfloat16),
-        in_specs=[
-            pl.BlockSpec(memory_space=pltpu.SMEM),
-            pl.BlockSpec(memory_space=pltpu.VMEM),
-            pl.BlockSpec(memory_space=pltpu.VMEM),
-        ],
-        out_specs=pl.BlockSpec(memory_space=pltpu.VMEM),
-        compiler_params=pltpu.CompilerParams(vmem_limit_bytes=32 * 2**20),
-        cost_estimate=pl.CostEstimate(
-            flops=2 * rows * every_key.shape[0] * (2 * LAT + ROPE),
-            bytes_accessed=rows * (2 * LAT + ROPE) * 2 + every_key.size * 2,
-            transcendentals=rows * every_key.shape[0],
-        ),
-        name="attend",
-    )(offsets, queries.reshape(rows, LAT + ROPE), every_key)
-    return out.reshape(queries.shape[0], H * LAT)
-
-
 def expert_kernel(
     n, owners,
-    table_ref, tokens_ref, gate_hbm, up_hbm, down_hbm, out_ref,
+    offset_ref, query_ref, latent_ref, table_ref, tokens_ref, gate_hbm, up_hbm, down_hbm,
+    attention_ref, out_ref,
+    keys, kz_ssem, kz_rsem, kx_ssem, kx_rsem, kc_ssem, kc_rsem, ordered, mixture,
     gate_w, up_w, down_w, w_sem,
     tables, tokens, t_ssem, t_rsem, x_rows,
     keep, core_send, core_recv, c_ssem, c_rsem,
@@ -80,6 +39,8 @@
     pairs = held // 2
     nz = n // 4
     subs = nz // pairs
+    block_rows = latent_ref.shape[0]
+    query_count = query_ref.shape[0]
     row_blocks = half // 16
     col_blocks = subs // row_blocks
     width = ff // col_blocks
@@ -152,6 +113,79 @@
         send(table_ref, tables.at[exp], t_ssem.at[0, k], t_rsem.at[0, exp], device)
         send(tokens_ref, tokens.at[exp], t_ssem.at[1, k], t_rsem.at[1, exp], device)
 
+    def keys_at(where, slot_side, slot_core):
+        start = (where * 4 + slot_side * 2 + slot_core) * block_rows
+        return keys.at[pl.ds(pl.multiple_of(start, 16), block_rows)]
+
+    own_keys = keys_at(far, side, core)
+    own_keys[...] = latent_ref[...]
+    for k in range(1, nz):
+        send(own_keys, own_keys, kz_ssem.at[k], kz_rsem.at[far], at_far(far_of(k)))
+
+    def keys_here(k):
+        where = far_of(nz - k) if k else far
+        here = keys_at(where, side, core)
+        if k:
+            arrived(here, kz_rsem.at[where])
+        send(here, here, kx_ssem.at[k], kx_rsem.at[where], beside)
+        send(here, here, kc_ssem.at[0, k], kc_rsem.at[0, where], sibling)
+
+    def keys_beside(k):
+        where = far_of(nz - k) if k else far
+        here = keys_at(where, 1 - side, core)
+        arrived(here, kx_rsem.at[where])
+        send(here, here, kc_ssem.at[1, k], kc_rsem.at[1, where], sibling)
+
+    def keys_complete():
+        for where in range(nz):
+            for j in range(2):
+                slot_side = side if j == 0 else 1 - side
+                arrived(keys_at(where, slot_side, 1 - core), kc_rsem.at[j, where])
+
+    keys_here(0)
+
+    wide = 2 * (LAT + ROPE)
+    pair_rows = 2 * query_count
+
+    @pl.loop(0, H // 2)
+    def _(at):
+        two = query_ref[:, pl.ds(pl.multiple_of(at * wide, 128), wide)].astype(jnp.float32)
+        ordered[pl.ds(pl.multiple_of(at * pair_rows, 8), pair_rows), :] = jnp.concatenate(
+            [two[:, : LAT + ROPE], two[:, LAT + ROPE :]], axis=0
+        )
+
+    def attend(chunk):
+        height = mixture.shape[0]
+        scores = (
+            lax.dot_general(
+                ordered[chunk * height : (chunk + 1) * height, :].astype(jnp.bfloat16),
+                keys[...],
+                (((1,), (1,)), ((), ())),
+                preferred_element_type=jnp.float32,
+            )
+            * softmax_scale
+        )
+        key_pos = lax.broadcasted_iota(jnp.int32, scores.shape, 1)
+        query_pos = offset_ref[0] + lax.rem(
+            lax.broadcasted_iota(jnp.int32, (height, 1), 0), query_count
+        )
+        scores = jnp.where(key_pos <= query_pos, scores, -jnp.inf)
+        weights = jnp.exp(scores - jnp.max(scores, axis=1, keepdims=True))
+        denominator = jnp.sum(weights, axis=1, keepdims=True)
+        mixed = jnp.dot(
+            weights.astype(jnp.bfloat16), keys[:, :LAT], preferred_element_type=jnp.float32
+        )
+        mixture[...] = mixed / denominator
+
+        @pl.loop(0, height // pair_rows)
+        def _(at):
+            two = mixture[pl.ds(pl.multiple_of(at * pair_rows, 8), pair_rows), :]
+            start = (chunk * (height // pair_rows) + at) * 2 * LAT
+            for k in range(2):
+                attention_ref[:, pl.ds(pl.multiple_of(start + k * LAT, 128), LAT)] = two[
+                    k * query_count : (k + 1) * query_count
+                ].astype(attention_ref.dtype)
+
     first = exp * held
     expert_ids = (lax.broadcasted_iota(jnp.int32, (held, count), 0) + first).astype(jnp.float32)
     earlier = (
@@ -197,18 +231,15 @@
             for k, weight in ((0, gate_w), (1, up_w)):
                 weight_copies[i, j][k].wait()
                 columns = slice(k * ff, (k + 1) * ff)
-                held_w = weight[expert]
-                core_send[i, j, :, columns] = jnp.dot(
-                    x_rows[expert, other, :], held_w, preferred_element_type=jnp.float32
-                ).astype(jnp.bfloat16)
                 keep[i, j, :, columns] = jnp.dot(
-                    x_rows[expert, mine, :], held_w, preferred_element_type=jnp.float32
+                    x_rows[expert], weight[expert], preferred_element_type=jnp.float32
                 )
+            core_send[i, j] = keep[i, j, other, :].astype(jnp.bfloat16)
             send(core_send.at[i, j], core_recv.at[i, j], c_ssem.at[i, j], c_rsem.at[i, j], sibling)
 
     def to_side(i):
         arrived(core_recv.at[i, 0], c_rsem.at[i, 0])
-        side_send[i] = (keep[i, 0] + core_recv[i, 0].astype(jnp.float32)).astype(jnp.bfloat16)
+        side_send[i] = (keep[i, 0, mine, :] + core_recv[i, 0].astype(jnp.float32)).astype(jnp.bfloat16)
         send(side_send.at[i], side_recv.at[i], s_ssem.at[i], s_rsem.at[i], beside)
 
     def block(i, sub):
@@ -219,7 +250,7 @@
         arrived(core_recv.at[i, 1], c_rsem.at[i, 1])
         arrived(side_recv.at[i], s_rsem.at[i])
         total = (
-            keep[i, 1] + core_recv[i, 1].astype(jnp.float32) + side_recv[i].astype(jnp.float32)
+            keep[i, 1, mine, :] + core_recv[i, 1].astype(jnp.float32) + side_recv[i].astype(jnp.float32)
         )
         for r in range(row_blocks):
             for c in range(col_blocks):
@@ -237,13 +268,27 @@
                 far_send.at[i, sub], far_recv.at[far], f_ssem.at[i, s], f_rsem.at[far], at_far(dest)
             )
 
+    forwards = [functools.partial(keys_here, k) for k in range(1, nz)]
+    forwards += [functools.partial(keys_beside, k) for k in range(nz)]
+    chunks = ordered.shape[0] // mixture.shape[0]
+    share = -(-len(forwards) // max(pairs - 1, 1))
     for t in range(pairs + 2):
         if t < pairs:
             multiply(t)
+        if t == pairs:
+            keys_complete()
+            attend(0)
+        if t == pairs + 1:
+            attend(1)
         if 0 <= t - 1 < pairs:
             to_side(t - 1)
         if 0 <= t - 2 < pairs:
             to_far(t - 2)
+        if t < pairs:
+            for forward in forwards[max(t - 1, 0) * share : t * share] if pairs > 1 else forwards:
+                forward()
+    for chunk in range(2, chunks):
+        attend(chunk)
 
     total = own[lax.rem(far, subs)]
     for k in range(1, nz):
@@ -292,8 +337,11 @@
                         )
                     )
             down_copies[d, j].wait()
-            made = jnp.dot(
-                jnp.concatenate(strips, axis=0), down_w[expert], preferred_element_type=jnp.float32
+            made = lax.dot_general(
+                jnp.concatenate(strips, axis=0),
+                down_w[expert],
+                (((1,), (1,)), ((), ())),
+                preferred_element_type=jnp.float32,
             ).astype(jnp.bfloat16)
             for s in range(owners):
                 result[s, pl.ds(pl.multiple_of(expert * CAP, CAP), CAP), :] = made[
@@ -329,7 +377,7 @@
         copy.wait_send()
 
 
-def experts(moe_input, routes, gate_values, w_gate, w_up, w_down):
+def layer(queries, latents, offsets, moe_input, routes, gate_values, w_gate, w_up, w_down):
     n, owners = lax.axis_size("ctx"), lax.axis_size("exp")
     held, depth, ff = w_gate.shape
     count, local_width = moe_input.shape
@@ -346,12 +394,15 @@
     bf16, f32 = jnp.bfloat16, jnp.float32
     vm = pltpu.VMEM
     scratch = [
-        vm((held, depth, ff), bf16), vm((held, depth, ff), bf16), vm((held, ff, depth), bf16),
+        vm((n * latents.shape[0], LAT + ROPE), bf16),
+        dma((nz,)), dma((nz,)), dma((nz,)), dma((nz,)), dma((2, nz)), dma((2, nz)),
+        vm((queries.shape[0] * H, LAT + ROPE), f32), vm((128, LAT), f32),
+        vm((held, depth, ff), bf16), vm((held, depth, ff), bf16), vm((held, depth, ff), bf16),
         dma((3, pairs, 2)),
         vm((owners, 16, 128), f32), vm((owners, count, local_width), bf16),
         dma((2, owners)), dma((2, owners)),
         vm((held, owners * CAP, local_width), bf16),
-        vm((pairs, 2, half, 2 * ff), f32), vm((pairs, 2, half, 2 * ff), bf16),
+        vm((pairs, 2, 2 * half, 2 * ff), f32), vm((pairs, 2, half, 2 * ff), bf16),
         vm((pairs, 2, half, 2 * ff), bf16), dma((pairs, 2)), dma((pairs, 2)),
         vm((pairs, half, 2 * ff), bf16), vm((pairs, half, 2 * ff), bf16), dma((pairs,)), dma((pairs,)),
         vm((pairs, subs, 16, 2 * width), bf16), vm((nz, 16, 2 * width), bf16),
@@ -366,9 +417,15 @@
     in_vmem = pl.BlockSpec(memory_space=pltpu.VMEM)
     return pl.pallas_call(
         functools.partial(expert_kernel, n, owners),
-        out_shape=jax.ShapeDtypeStruct(moe_input.shape, moe_input.dtype),
-        in_specs=[in_vmem, in_vmem, any_space, any_space, any_space],
-        out_specs=in_vmem,
+        out_shape=[
+            jax.ShapeDtypeStruct((queries.shape[0], H * LAT), bf16),
+            jax.ShapeDtypeStruct(moe_input.shape, bf16),
+        ],
+        in_specs=[
+            pl.BlockSpec(memory_space=pltpu.SMEM), in_vmem, in_vmem, in_vmem, in_vmem,
+            any_space, any_space, any_space,
+        ],
+        out_specs=[in_vmem, in_vmem],
         scratch_shapes=scratch,
         compiler_params=pltpu.CompilerParams(
             collective_id=0, has_side_effects=True, vmem_limit_bytes=56 * 2**20
@@ -378,20 +435,13 @@
             bytes_accessed=3 * held * depth * ff * 2,
             transcendentals=0,
         ),
-        name="experts",
-    )(table, moe_input, w_gate, w_up, w_down)
-
-
-def local(queries, latents, offsets, moe_input, routes, gate_values, w_gate, w_up, w_down):
-    every_key = lax.all_gather(latents, "ctx", axis=0, tiled=True)
-    moe_output = experts(moe_input, routes, gate_values, w_gate, w_up, w_down)
-    attention_out = attend(queries, every_key, offsets)
-    return (attention_out, moe_output)
+        name="layer",
+    )(offsets, queries, latents, table, moe_input, w_gate, w_up, jnp.swapaxes(w_down, 1, 2))
 
 
 def solution(mesh):
     return jax.shard_map(
-        local,
+        lambda *operands: tuple(layer(*operands)),
         mesh=mesh,
         in_specs=(
             P(("ctx", "exp"), None),

time: 86.7 us -> 61.9 us (0.71)
  between operations: 14.7 us -> 1.29 us
  local copies, waits for them, and re-layouts: 16.3 us -> 3.36 us
  other arithmetic: 0.61 us -> 1.98 us
  Pallas kernels: 53.8 us -> 55 us
    unnamed x10 -> x2, local copies, waits for them, and re-layouts: 14.5 us -> 3.36 us
    reshape x2 -> x0, local copies, waits for them, and re-layouts: 1.83 us -> none  [the longest x1 1.18 us: attend(): return out.reshape(queries.shape[0], H * LAT)]
    pallas_call x2 -> x1, Pallas kernels: 53.8 us -> 55 us  [layer(): pl.pallas_call(functools.partial(expert_kernel, n, owners), out_shape=[ja...]
  transfers between devices with their start and end apart: 1 -> 0, of which waited for: 0 -> 0; matrix products, arithmetic and copies ran while one was open for 15% -> 0% of each run, Pallas kernels for 57% -> 0%
where the time goes in v2:
time: 61.9 us; the launch traced here: 61.6 us
  Pallas kernels  55 us (89%)
  local copies, waits for them, and re-layouts  3.36 us (5%)
  other arithmetic  1.98 us (3%)
  between operations  1.29 us (2%)
    pallas_call x1, Pallas kernels, layer(): pl.pallas_call(functools.partial(expert_kernel, n, owners), out_shape=[ja...  55 us
    unnamed x2, local copies, waits for them, and re-layouts  3.36 us
    concatenate x1, other arithmetic, layer(): jnp.concatenate([jnp.pad(routes.T.astype(jnp.float32), pad), jnp.pad(gate...  1.29 us

profile of v2, /device:TPU:0, one launch (start us, length us, event | category | flops | bytes accessed | tf_op | source)
XLA Modules:
  0.0 61.6 jit_solution(2930906592006608139)
XLA Ops:
  1.3 0.7 %convert_bitcast_fusion = f32[6,32]{1,0:T(8,128)S(1)} fusion(s32[32,6]{0,1:T(8,128)} %param.13), kind=kLoop, calls=%fused_computation.3 | loop fusion | flops 192 | bytes 1536 | tf_op jit(solution)/shard_map/convert_element_type | solution.py:386
  2.0 1.3 %select_maximum_fusion.table_ref = f32[16,128]{1,0:T(8,128)} fusion(f32[6,32]{1,0:T(8,128)} %bitcast.5, f32[6,32]{1,0:T(8,128)S(1)} %convert_bitcast_fusion), kind=kLoop, calls=%fused_computation | loop fusion | flops 10240 | bytes 9728 | tf_op jit(solution)/shard_map/concatenate | solution.py:385
  3.3 55.0 %layer.1 = (bf16[4,65536]{1,0:T(4,128)(2,1)}, bf16[32,320]{1,0:T(8,128)(2,1)}) custom-call(s32[1]{0:T(128)S(6)} %copy.13.offset_ref, bf16[4,73728]{1,0:T(4,128)(2,1)} %query_ref.1, bf16[80,576]{1,0:T(8,128)(2,1)} %latent_ref.1, f32[16,128]{1,0:T(8,128)} %select_maximum_fusion.table_ref, bf16[32,320]{1,0:T(8,128)(2,1)} %tokens_ref.1, ...), custom_call_target="tpu_custom_call" | custom-call | flops 754974720 | bytes 23592960 | tf_op jit(solution)/shard_map/layer/pallas_call | solution.py:418
  58.2 2.0 %copy.14 = bf16[4,65536]{1,0:T(4,128)(2,1)} copy(bf16[4,65536]{1,0:T(4,128)(2,1)} %get-tuple-element.4) | data formatting | bytes 1048576
  60.2 1.3 %copy.15 = bf16[32,320]{1,0:T(8,128)(2,1)} copy(bf16[32,320]{1,0:T(8,128)(2,1)} %get-tuple-element.5) | data formatting | bytes 40960

commit v3 on v2

--- a/solution.py
+++ b/solution.py
@@ -20,9 +20,9 @@
 
 def expert_kernel(
     n, owners,
-    offset_ref, query_ref, latent_ref, table_ref, tokens_ref, gate_hbm, up_hbm, down_hbm,
+    offset_ref, query_ref, latent_ref, routes_ref, gates_ref, tokens_ref, gate_hbm, up_hbm, down_hbm,
     attention_ref, out_ref,
-    keys, kz_ssem, kz_rsem, kx_ssem, kx_rsem, kc_ssem, kc_rsem, ordered, mixture,
+    table, keys, kz_ssem, kz_rsem, kx_ssem, kx_rsem, kc_ssem, kc_rsem, ordered, mixture,
     gate_w, up_w, down_w, w_sem,
     tables, tokens, t_ssem, t_rsem, x_rows,
     keep, core_send, core_recv, c_ssem, c_rsem,
@@ -71,8 +71,6 @@
                 pltpu.make_async_copy(hbm.at[expert], vmem.at[expert], w_sem.at[k, i, j])
                 for k, (hbm, vmem) in enumerate(((gate_hbm, gate_w), (up_hbm, up_w)))
             ]
-            for copy in weight_copies[i, j]:
-                copy.start()
     down_order = [(d, j) for d in range(pairs) for j in range(2)]
     down_expert = {}
     down_copies = {}
@@ -82,7 +80,18 @@
         down_copies[d, j] = pltpu.make_async_copy(
             down_hbm.at[expert], down_w.at[expert], w_sem.at[2, d, j]
         )
-        down_copies[d, j].start()
+
+    def start_weights(i):
+        for j in range(2):
+            for copy in weight_copies[i, j]:
+                copy.start()
+
+    for i in range(min(2, pairs)):
+        start_weights(i)
+
+    table[...] = jnp.zeros_like(table)
+    table[:TOPK, :count] = routes_ref[...].astype(jnp.float32)
+    table[8 : 8 + TOPK, :count] = gates_ref[...]
 
     barrier = pltpu.get_barrier_semaphore()
     greeted = [sibling, beside]
@@ -110,7 +119,7 @@
 
     for k in range(1, owners):
         device = (ctx, owner_of(k))
-        send(table_ref, tables.at[exp], t_ssem.at[0, k], t_rsem.at[0, exp], device)
+        send(table, tables.at[exp], t_ssem.at[0, k], t_rsem.at[0, exp], device)
         send(tokens_ref, tokens.at[exp], t_ssem.at[1, k], t_rsem.at[1, exp], device)
 
     def keys_at(where, slot_side, slot_core):
@@ -147,12 +156,13 @@
     wide = 2 * (LAT + ROPE)
     pair_rows = 2 * query_count
 
-    @pl.loop(0, H // 2)
-    def _(at):
-        two = query_ref[:, pl.ds(pl.multiple_of(at * wide, 128), wide)].astype(jnp.float32)
-        ordered[pl.ds(pl.multiple_of(at * pair_rows, 8), pair_rows), :] = jnp.concatenate(
-            [two[:, : LAT + ROPE], two[:, LAT + ROPE :]], axis=0
-        )
+    def order_queries():
+        @pl.loop(0, H // 2, unroll=4)
+        def _(at):
+            two = query_ref[:, pl.ds(pl.multiple_of(at * wide, 128), wide)].astype(jnp.float32)
+            ordered[pl.ds(pl.multiple_of(at * pair_rows, 8), pair_rows), :] = jnp.concatenate(
+                [two[:, : LAT + ROPE], two[:, LAT + ROPE :]], axis=0
+            )
 
     def attend(chunk):
         height = mixture.shape[0]
@@ -177,7 +187,7 @@
         )
         mixture[...] = mixed / denominator
 
-        @pl.loop(0, height // pair_rows)
+        @pl.loop(0, height // pair_rows, unroll=4)
         def _(at):
             two = mixture[pl.ds(pl.multiple_of(at * pair_rows, 8), pair_rows), :]
             start = (chunk * (height // pair_rows) + at) * 2 * LAT
@@ -194,13 +204,13 @@
     ).astype(jnp.bfloat16)
     slots = lax.broadcasted_iota(jnp.int32, (held, CAP, count), 1).astype(jnp.float32)
 
-    def placement(table):
+    def placement(listed):
         named = jnp.zeros((held, count), jnp.float32)
         gates = jnp.zeros((held, count), jnp.float32)
         for k in range(TOPK):
-            hit = table[k : k + 1, :count] == expert_ids
+            hit = listed[k : k + 1, :count] == expert_ids
             named = jnp.where(hit, 1.0, named)
-            gates = jnp.where(hit, table[8 + k : 9 + k, :count], gates)
+            gates = jnp.where(hit, listed[8 + k : 9 + k, :count], gates)
         rank = jnp.dot(named.astype(jnp.bfloat16), earlier, preferred_element_type=jnp.float32)
         rank = jnp.where(named > 0.5, rank, -1.0)
         picked = rank[:, None, :] == slots
@@ -208,14 +218,14 @@
         weighted = jnp.where(picked, gates[:, None, :], 0.0).reshape(held * CAP, count)
         return chosen.astype(jnp.bfloat16), weighted
 
-    def place(table, values, owner):
-        chosen, weighted = placement(table)
+    def place(listed, values, owner):
+        chosen, weighted = placement(listed)
         placed = jnp.dot(chosen, values, preferred_element_type=jnp.float32).astype(jnp.bfloat16)
         for e in range(held):
             x_rows[e, pl.ds(pl.multiple_of(owner * CAP, CAP), CAP), :] = placed[e * CAP : (e + 1) * CAP]
         return weighted
 
-    weighted_of = {0: place(table_ref[...], tokens_ref[...], exp)}
+    weighted_of = {0: place(table[...], tokens_ref[...], exp)}
     for k in range(1, owners):
         owner = owner_of(k)
         arrived(tables.at[owner], t_rsem.at[0, owner])
@@ -226,6 +236,11 @@
     other = pl.ds(pl.multiple_of((1 - core) * half, 16), half)
 
     def multiply(i):
+        if i + 2 < pairs:
+            start_weights(i + 2)
+        if i == max(pairs - 2, 0):
+            for key in down_order:
+                down_copies[key].start()
         for j in range(2):
             expert = pair_of[i] * 2 + (1 - side if j == 0 else side)
             for k, weight in ((0, gate_w), (1, up_w)):
@@ -272,23 +287,22 @@
     forwards += [functools.partial(keys_beside, k) for k in range(nz)]
     chunks = ordered.shape[0] // mixture.shape[0]
     share = -(-len(forwards) // max(pairs - 1, 1))
-    for t in range(pairs + 2):
-        if t < pairs:
-            multiply(t)
-        if t == pairs:
-            keys_complete()
-            attend(0)
-        if t == pairs + 1:
-            attend(1)
-        if 0 <= t - 1 < pairs:
+    for t in range(pairs):
+        multiply(t)
+        if t:
             to_side(t - 1)
-        if 0 <= t - 2 < pairs:
-            to_far(t - 2)
-        if t < pairs:
-            for forward in forwards[max(t - 1, 0) * share : t * share] if pairs > 1 else forwards:
-                forward()
-    for chunk in range(2, chunks):
+        for forward in forwards[max(t - 1, 0) * share : t * share] if pairs > 1 else forwards:
+            forward()
+    to_side(pairs - 1)
+    to_far(0)
+    order_queries()
+    for t in range(1, pairs - 1):
+        to_far(t)
+    keys_complete()
+    for chunk in range(chunks):
         attend(chunk)
+        if chunk == 0 and pairs > 1:
+            to_far(pairs - 1)
 
     total = own[lax.rem(far, subs)]
     for k in range(1, nz):
@@ -381,10 +395,6 @@
     n, owners = lax.axis_size("ctx"), lax.axis_size("exp")
     held, depth, ff = w_gate.shape
     count, local_width = moe_input.shape
-    pad = ((0, 8 - TOPK), (0, 128 - count))
-    table = jnp.concatenate(
-        [jnp.pad(routes.T.astype(jnp.float32), pad), jnp.pad(gate_values.T, pad)], axis=0
-    )
     half = owners * CAP // 2
     pairs = held // 2
     nz = n // 4
@@ -394,7 +404,7 @@
     bf16, f32 = jnp.bfloat16, jnp.float32
     vm = pltpu.VMEM
     scratch = [
-        vm((n * latents.shape[0], LAT + ROPE), bf16),
+        vm((16, 128), f32), vm((n * latents.shape[0], LAT + ROPE), bf16),
         dma((nz,)), dma((nz,)), dma((nz,)), dma((nz,)), dma((2, nz)), dma((2, nz)),
         vm((queries.shape[0] * H, LAT + ROPE), f32), vm((128, LAT), f32),
         vm((held, depth, ff), bf16), vm((held, depth, ff), bf16), vm((held, depth, ff), bf16),
@@ -422,7 +432,7 @@
             jax.ShapeDtypeStruct(moe_input.shape, bf16),
         ],
         in_specs=[
-            pl.BlockSpec(memory_space=pltpu.SMEM), in_vmem, in_vmem, in_vmem, in_vmem,
+            pl.BlockSpec(memory_space=pltpu.SMEM), in_vmem, in_vmem, in_vmem, in_vmem, in_vmem,
             any_space, any_space, any_space,
         ],
         out_specs=[in_vmem, in_vmem],
@@ -436,7 +446,10 @@
             transcendentals=0,
         ),
         name="layer",
-    )(offsets, queries, latents, table, moe_input, w_gate, w_up, jnp.swapaxes(w_down, 1, 2))
+    )(
+        offsets, queries, latents, routes.T, gate_values.T, moe_input,
+        w_gate, w_up, jnp.swapaxes(w_down, 1, 2),
+    )
 
 
 def solution(mesh):

time: 61.9 us -> 56.7 us (0.916)
  Pallas kernels: 55 us -> 51.8 us
  other arithmetic: 1.98 us -> 0 us
    pallas_call x1, Pallas kernels: 55 us -> 51.8 us  [layer(): pl.pallas_call(functools.partial(expert_kernel, n, owners), out_shape=[ja...]
    concatenate x1 -> x0, other arithmetic: 1.29 us -> none  [layer(): jnp.concatenate([jnp.pad(routes.T.astype(jnp.float32), pad), jnp.pad(gate...]
    convert_element_type x1 -> x0, other arithmetic: 0.69 us -> none  [layer(): routes.T.astype(jnp.float32)]
where the time goes in v3:
time: 56.7 us; the launch traced here: 56.4 us
  Pallas kernels  51.8 us (91%)
  local copies, waits for them, and re-layouts  3.36 us (6%)
  between operations  1.29 us (2%)
    pallas_call x1, Pallas kernels, layer(): pl.pallas_call(functools.partial(expert_kernel, n, owners), out_shape=[ja...  51.8 us
    unnamed x2, local copies, waits for them, and re-layouts  3.36 us

profile of v3, /device:TPU:0, one launch (start us, length us, event | category | flops | bytes accessed | tf_op | source)
XLA Modules:
  0.0 56.4 jit_solution(4040970755590485519)
XLA Ops:
  1.3 51.8 %layer.1 = (bf16[4,65536]{1,0:T(4,128)(2,1)}, bf16[32,320]{1,0:T(8,128)(2,1)}) custom-call(s32[1]{0:T(128)S(6)} %copy.13.offset_ref, bf16[4,73728]{1,0:T(4,128)(2,1)} %query_ref.1, bf16[80,576]{1,0:T(8,128)(2,1)} %latent_ref.1, s32[6,32]{1,0:T(8,128)} %bitcast.4, f32[6,32]{1,0:T(8,128)} %bitcast.5, bf16[32,320]{1,0:T(8,128)(2,1)} %tokens_ref.1, ...), custom_call_target="tpu_custom_call" | custom-call | flops 754974720 | bytes 23592960 | tf_op jit(solution)/shard_map/layer/pallas_call | solution.py:428
  53.1 2.0 %copy.14 = bf16[4,65536]{1,0:T(4,128)(2,1)} copy(bf16[4,65536]{1,0:T(4,128)(2,1)} %get-tuple-element.4) | data formatting | bytes 1048576
  55.1 1.3 %copy.15 = bf16[32,320]{1,0:T(8,128)(2,1)} copy(bf16[32,320]{1,0:T(8,128)(2,1)} %get-tuple-element.5) | data formatting | bytes 40960

commit v4 on v3

--- a/solution.py
+++ b/solution.py
@@ -22,7 +22,7 @@
     n, owners,
     offset_ref, query_ref, latent_ref, routes_ref, gates_ref, tokens_ref, gate_hbm, up_hbm, down_hbm,
     attention_ref, out_ref,
-    table, keys, kz_ssem, kz_rsem, kx_ssem, kx_rsem, kc_ssem, kc_rsem, ordered, mixture,
+    table, keys, kz_ssem, kz_rsem, kx_ssem, kx_rsem, kc_ssem, kc_rsem, ky_ssem, ky_rsem, ordered, mixture,
     gate_w, up_w, down_w, w_sem,
     tables, tokens, t_ssem, t_rsem, x_rows,
     keep, core_send, core_recv, c_ssem, c_rsem,
@@ -126,32 +126,70 @@
         start = (where * 4 + slot_side * 2 + slot_core) * block_rows
         return keys.at[pl.ds(pl.multiple_of(start, 16), block_rows)]
 
+    shared = owners == 2
+    active = core == exp
+    across = (ctx, owner_of(1))
+    sent_active = []
+
+    def if_active(body):
+        if shared:
+            pl.when(active)(body)
+        else:
+            body()
+
+    def remote(src, ssem, rsem, device):
+        copy = pltpu.make_async_remote_copy(
+            src_ref=src, dst_ref=src, send_sem=ssem, recv_sem=rsem,
+            device_id=device, device_id_type=MESH,
+        )
+        sent_active.append(copy)
+        return copy
+
     own_keys = keys_at(far, side, core)
-    own_keys[...] = latent_ref[...]
-    for k in range(1, nz):
-        send(own_keys, own_keys, kz_ssem.at[k], kz_rsem.at[far], at_far(far_of(k)))
-
-    def keys_here(k):
+    own_copies = [
+        remote(own_keys, kz_ssem.at[k], kz_rsem.at[far], at_far(far_of(k))) for k in range(1, nz)
+    ]
+
+    @if_active
+    def _():
+        own_keys[...] = latent_ref[...]
+        for copy in own_copies:
+            copy.start()
+
+    def keys_step(j, k):
         where = far_of(nz - k) if k else far
-        here = keys_at(where, side, core)
-        if k:
-            arrived(here, kz_rsem.at[where])
-        send(here, here, kx_ssem.at[k], kx_rsem.at[where], beside)
-        send(here, here, kc_ssem.at[0, k], kc_rsem.at[0, where], sibling)
-
-    def keys_beside(k):
-        where = far_of(nz - k) if k else far
-        here = keys_at(where, 1 - side, core)
-        arrived(here, kx_rsem.at[where])
-        send(here, here, kc_ssem.at[1, k], kc_rsem.at[1, where], sibling)
+        here = keys_at(where, side if j == 0 else 1 - side, core)
+        copies = []
+        if j == 0:
+            copies.append(remote(here, kx_ssem.at[k], kx_rsem.at[where], beside))
+        if shared:
+            copies.append(remote(here, ky_ssem.at[j, k], ky_rsem.at[j, where], across))
+
+        @if_active
+        def _():
+            if j == 0 and k:
+                arrived(here, kz_rsem.at[where])
+            if j == 1:
+                arrived(here, kx_rsem.at[where])
+            for copy in copies:
+                copy.start()
+
+        if shared:
+
+            @pl.when(jnp.logical_not(active))
+            def _():
+                arrived(here, ky_rsem.at[j, where])
+
+        send(here, here, kc_ssem.at[j, k], kc_rsem.at[j, where], sibling)
+
+    keys_here = functools.partial(keys_step, 0)
+    keys_beside = functools.partial(keys_step, 1)
 
     def keys_complete():
         for where in range(nz):
             for j in range(2):
                 slot_side = side if j == 0 else 1 - side
                 arrived(keys_at(where, slot_side, 1 - core), kc_rsem.at[j, where])
-
-    keys_here(0)
 
     wide = 2 * (LAT + ROPE)
     pair_rows = 2 * query_count
@@ -283,11 +321,13 @@
                 far_send.at[i, sub], far_recv.at[far], f_ssem.at[i, s], f_rsem.at[far], at_far(dest)
             )
 
-    forwards = [functools.partial(keys_here, k) for k in range(1, nz)]
+    forwards = [functools.partial(keys_here, k) for k in range(nz)]
     forwards += [functools.partial(keys_beside, k) for k in range(nz)]
     chunks = ordered.shape[0] // mixture.shape[0]
-    share = -(-len(forwards) // max(pairs - 1, 1))
+    share = -(-(len(forwards) - 1) // max(pairs - 1, 1))
     for t in range(pairs):
+        if t == 0:
+            forwards.pop(0)()
         multiply(t)
         if t:
             to_side(t - 1)
@@ -390,6 +430,11 @@
     for copy in sent:
         copy.wait_send()
 
+    @if_active
+    def _():
+        for copy in sent_active:
+            copy.wait_send()
+
 
 def layer(queries, latents, offsets, moe_input, routes, gate_values, w_gate, w_up, w_down):
     n, owners = lax.axis_size("ctx"), lax.axis_size("exp")
@@ -406,6 +451,7 @@
     scratch = [
         vm((16, 128), f32), vm((n * latents.shape[0], LAT + ROPE), bf16),
         dma((nz,)), dma((nz,)), dma((nz,)), dma((nz,)), dma((2, nz)), dma((2, nz)),
+        dma((2, nz)), dma((2, nz)),
         vm((queries.shape[0] * H, LAT + ROPE), f32), vm((128, LAT), f32),
         vm((held, depth, ff), bf16), vm((held, depth, ff), bf16), vm((held, depth, ff), bf16),
         dma((3, pairs, 2)),

time: 56.7 us -> 58.7 us (1.035)
  Pallas kernels: 51.8 us -> 53.7 us
    pallas_call x1, Pallas kernels: 51.8 us -> 53.7 us  [layer(): pl.pallas_call(functools.partial(expert_kernel, n, owners), out_shape=[ja...]
where the time goes in v4:
time: 58.7 us; the launch traced here: 58.4 us
  Pallas kernels  53.7 us (91%)
  local copies, waits for them, and re-layouts  3.36 us (6%)
  between operations  1.29 us (2%)
    pallas_call x1, Pallas kernels, layer(): pl.pallas_call(functools.partial(expert_kernel, n, owners), out_shape=[ja...  53.7 us
    unnamed x2, local copies, waits for them, and re-layouts  3.36 us

profile of v4, /device:TPU:0, one launch (start us, length us, event | category | flops | bytes accessed | tf_op | source)
XLA Modules:
  0.0 58.4 jit_solution(4691309911676384100)
XLA Ops:
  1.3 53.7 %layer.1 = (bf16[4,65536]{1,0:T(4,128)(2,1)}, bf16[32,320]{1,0:T(8,128)(2,1)}) custom-call(s32[1]{0:T(128)S(6)} %copy.13.offset_ref, bf16[4,73728]{1,0:T(4,128)(2,1)} %query_ref.1, bf16[80,576]{1,0:T(8,128)(2,1)} %latent_ref.1, s32[6,32]{1,0:T(8,128)} %bitcast.4, f32[6,32]{1,0:T(8,128)} %bitcast.5, bf16[32,320]{1,0:T(8,128)(2,1)} %tokens_ref.1, ...), custom_call_target="tpu_custom_call" | custom-call | flops 754974720 | bytes 23592960 | tf_op jit(solution)/shard_map/layer/pallas_call | solution.py:474
  55.0 2.0 %copy.14 = bf16[4,65536]{1,0:T(4,128)(2,1)} copy(bf16[4,65536]{1,0:T(4,128)(2,1)} %get-tuple-element.4) | data formatting | bytes 1048576
  57.0 1.3 %copy.15 = bf16[32,320]{1,0:T(8,128)(2,1)} copy(bf16[32,320]{1,0:T(8,128)(2,1)} %get-tuple-element.5) | data formatting | bytes 40960

commit v5 on v3

--- a/solution.py
+++ b/solution.py
@@ -286,23 +286,21 @@
     forwards = [functools.partial(keys_here, k) for k in range(1, nz)]
     forwards += [functools.partial(keys_beside, k) for k in range(nz)]
     chunks = ordered.shape[0] // mixture.shape[0]
-    share = -(-len(forwards) // max(pairs - 1, 1))
+    share = -(-len(forwards) // max(pairs - 2, 1))
     for t in range(pairs):
         multiply(t)
         if t:
             to_side(t - 1)
-        for forward in forwards[max(t - 1, 0) * share : t * share] if pairs > 1 else forwards:
+        for forward in forwards[max(t - 2, 0) * share : max(t - 1, 0) * share] if pairs > 2 else forwards * (t == 0):
             forward()
     to_side(pairs - 1)
     to_far(0)
     order_queries()
-    for t in range(1, pairs - 1):
+    for t in range(1, pairs):
         to_far(t)
     keys_complete()
-    for chunk in range(chunks):
+    for chunk in range(chunks // 2):
         attend(chunk)
-        if chunk == 0 and pairs > 1:
-            to_far(pairs - 1)
 
     total = own[lax.rem(far, subs)]
     for k in range(1, nz):
@@ -319,12 +317,15 @@
     mine_block = hidden.at[far, side, core]
     for k in range(1, nz):
         send(mine_block, mine_block, hz_ssem.at[k], hz_rsem.at[far], at_far(far_of(k)))
+    attend(chunks // 2)
     for k in range(nz):
         where = far_of(nz - k) if k else far
         if k:
             arrived(hidden.at[where, side, core], hz_rsem.at[where])
         pass_on(where, side, hx_ssem.at[k], hx_rsem.at[where], beside)
         pass_on(where, side, hc_ssem.at[0, k], hc_rsem.at[0, where], sibling)
+    for chunk in range(chunks // 2 + 1, chunks):
+        attend(chunk)
     for k in range(nz):
         where = far_of(nz - k) if k else far
         arrived(hidden.at[where, 1 - side, core], hx_rsem.at[where])

time: 56.7 us -> 57.7 us (1.018)
  Pallas kernels: 51.8 us -> 52.8 us
    pallas_call x1, Pallas kernels: 51.8 us -> 52.8 us  [layer(): pl.pallas_call(functools.partial(expert_kernel, n, owners), out_shape=[ja...]
where the time goes in v5:
time: 57.7 us; the launch traced here: 57.4 us
  Pallas kernels  52.8 us (92%)
  local copies, waits for them, and re-layouts  3.36 us (6%)
  between operations  1.29 us (2%)
    pallas_call x1, Pallas kernels, layer(): pl.pallas_call(functools.partial(expert_kernel, n, owners), out_shape=[ja...  52.8 us
    unnamed x2, local copies, waits for them, and re-layouts  3.36 us

profile of v5, /device:TPU:0, one launch (start us, length us, event | category | flops | bytes accessed | tf_op | source)
XLA Modules:
  0.0 57.4 jit_solution(5473598086961721519)
XLA Ops:
  1.3 52.8 %layer.1 = (bf16[4,65536]{1,0:T(4,128)(2,1)}, bf16[32,320]{1,0:T(8,128)(2,1)}) custom-call(s32[1]{0:T(128)S(6)} %copy.13.offset_ref, bf16[4,73728]{1,0:T(4,128)(2,1)} %query_ref.1, bf16[80,576]{1,0:T(8,128)(2,1)} %latent_ref.1, s32[6,32]{1,0:T(8,128)} %bitcast.4, f32[6,32]{1,0:T(8,128)} %bitcast.5, bf16[32,320]{1,0:T(8,128)(2,1)} %tokens_ref.1, ...), custom_call_target="tpu_custom_call" | custom-call | flops 754974720 | bytes 23592960 | tf_op jit(solution)/shard_map/layer/pallas_call | solution.py:429
  54.1 2.0 %copy.14 = bf16[4,65536]{1,0:T(4,128)(2,1)} copy(bf16[4,65536]{1,0:T(4,128)(2,1)} %get-tuple-element.4) | data formatting | bytes 1048576
  56.1 1.3 %copy.15 = bf16[32,320]{1,0:T(8,128)(2,1)} copy(bf16[32,320]{1,0:T(8,128)(2,1)} %get-tuple-element.5) | data formatting | bytes 40960
